TPU v7x, 768 devices: a whole 4x8x12 slice. The times are simulated.
768 devices in a mesh: row: 8 (over y_lo, x), rep: 96 (over y_hi, z, core).
Axes of the slice: x: 4, y: 8 (y_hi: 4, y_lo: 2; y = y_hi * 2 + y_lo), z: 12, core: 2. Of those that a mesh axis runs over, the one named last changes fastest.
Arguments:
- features: bfloat16 [196608, 256], P(('row', 'rep')), may hold values from -6 to 6
- weight: bfloat16 [256, 256], replicated, may hold values from -0.375 to 0.375
- bias: float32 [256], replicated, may hold values from -3 to 3
- tile_vals: bfloat16 [8, 96, 32, 128, 128], P('row', 'rep'), may hold values from -0.25 to 0.25
- tile_rows: int32 [8, 96, 32], P('row', 'rep'), may hold values from 0 to 15, as said below
- tile_cols: int32 [8, 96, 32], P('row', 'rep'), may hold values from 0 to 15, as said below
- tile_counts: int32 [8, 96], P('row', 'rep'), may hold values from 1 to 32, as said below
- grad_out: bfloat16 [196608, 256], P(('row', 'rep')), may hold values from -6 to 6
Outputs:
- activations: bfloat16 [196608, 256], P(('row', 'rep'))
- grad_features: bfloat16 [196608, 256], P(('row', 'rep'))
- grad_weight: float32 [256, 256], replicated
- grad_bias: float32 [256], replicated
Inputs may be any that keep to these rules, and one draw needn't show every extreme that they name: `tile_rows`: destination tile indices; within one device the first tile_counts slots name distinct (tile_rows, tile_cols) pairs, and slots at or past tile_counts are unused. `tile_cols`: source tile indices. `tile_counts`: live slots per device; some device has all 32 slots live.
All inputs are finite; a program needn't handle non-finite values.
Results may differ from a plain program's by a relative error of at most 0.013.
Values may be sent and summed in bfloat16 or wider, within the bound.
No kernel may reach another device: no remote copies, remote signals or barrier semaphores. Data moves between devices by JAX's collectives and lax.ppermute only.
A program may use at most 32 MiB of HBM per device.

v0:
```python
import jax
import jax.numpy as jnp
from jax import lax
from jax.sharding import PartitionSpec as P

K = 8


def passed_along(shard, axis, by):
    size = lax.axis_size(axis)
    return lax.ppermute(shard, axis, [(i, (i + by) % size) for i in range(size)])


def shards(features, weight, bias, tile_vals, tile_rows, tile_cols, tile_counts, grad_out):
    block = features.shape[0]
    width = features.shape[1]
    tile = tile_vals.shape[3]
    per_block = block // tile
    group_rows = lax.axis_size("row")
    vals = tile_vals[0, 0]
    rows = tile_rows[0, 0]
    cols = tile_cols[0, 0]
    slots = rows.shape[0]
    live = jnp.arange(slots, dtype=jnp.int32) < tile_counts[0, 0]
    dest_onehot = (
        (rows[None, :] == jnp.arange(K * per_block, dtype=jnp.int32)[:, None]) & live[None, :]
    ).astype(jnp.float32)
    source_onehot = (
        (cols[None, :] == jnp.arange(group_rows * per_block, dtype=jnp.int32)[:, None])
        & live[None, :]
    ).astype(jnp.float32)
    xw = jnp.dot(features, weight, preferred_element_type=jnp.float32).astype(jnp.bfloat16)
    gathered = lax.all_gather(xw, "row", axis=0, tiled=True)
    source = gathered.reshape(group_rows * per_block, tile, width)[cols]
    product = jnp.einsum("tij,tjh->tih", vals, source, preferred_element_type=jnp.float32)
    partial_sums = jnp.einsum("bt,tih->bih", dest_onehot, product).reshape(K, block, width)
    running = partial_sums[K - 1]
    for offset in range(K - 2, -1, -1):
        running = passed_along(running, "rep", 1) + partial_sums[offset]
    pre = running + bias[None, :]
    activations = jax.nn.silu(pre).astype(jnp.bfloat16)
    sig = jax.nn.sigmoid(pre)
    grad_pre = (grad_out.astype(jnp.float32) * sig * (1.0 + pre * (1.0 - sig))).astype(jnp.bfloat16)
    received = [grad_pre]
    current = grad_pre
    for offset in range(1, K):
        current = passed_along(current, "rep", -1)
        received.append(current)
    reached = jnp.stack(received, axis=0).reshape(K * per_block, tile, width)[rows]
    back_product = jnp.einsum("tij,tih->tjh", vals, reached, preferred_element_type=jnp.float32)
    source_terms = jnp.einsum("bt,tjh->bjh", source_onehot, back_product).reshape(
        group_rows * block, width
    )
    source_sum = lax.psum_scatter(source_terms, "row", scatter_dimension=0, tiled=True)
    source_grad = source_sum.astype(jnp.bfloat16)
    grad_features = jnp.dot(source_grad, weight.T, preferred_element_type=jnp.float32).astype(
        jnp.bfloat16
    )
    local_weight = lax.dot_general(
        features, source_grad, (((0,), (0,)), ((), ())), preferred_element_type=jnp.float32
    )
    local_bias = jnp.sum(grad_pre.astype(jnp.float32), axis=0)
    grad_weight, grad_bias = lax.psum((local_weight, local_bias), ("row", "rep"))
    return (activations, grad_features, grad_weight, grad_bias)


def solution(mesh):
    placed = (
        P(("row", "rep"), None),
        P(),
        P(),
        P("row", "rep", None, None, None),
        P("row", "rep", None),
        P("row", "rep", None),
        P("row", "rep"),
        P(("row", "rep"), None),
    )
    return jax.shard_map(
        shards,
        mesh=mesh,
        in_specs=placed,
        out_specs=(P(("row", "rep"), None), P(("row", "rep"), None), P(), P()),
        check_vma=False,
    )
```

profile of v0, /device:TPU:1, one launch (start us, length us, event | category | flops | bytes accessed | tf_op | source)
XLA Modules:
  0.0 832.5 jit_solution(11321999101261344174)
XLA Ops:
  10.5 50.2 %all-gather.2.cloned.1.call-done = bf16[2048,256]{1,0:T(8,128)(2,1)} async-done(((bf16[256,256]{1,0:T(8,128)(2,1)}), bf16[2048,256]{1,0:T(8,128)(2,1)}) %all-gather.2.cloned.1.call-update) | async-done | bytes 1048592 | tf_op jit(solution)/shard_map/all_gather | solution.py:33
  60.8 1.9 gather_fusion
  62.7 2.1 fusion.6
  64.8 3.4 copy.23
  69.4 8.6 %collective-permute-start = (f32[256,256]{1,0:T(8,128)S(1)}, f32[256,256]{1,0:T(8,128)S(1)}, u32[]{:S(2)}, u32[]{:S(2)}) collective-permute-start(f32[256,256]{1,0:T(8,128)S(1)} %bitcast.81), channel_id=1, source_target_pairs={{0,1},{1,2},{2,3},{3,4},{4,5},{5,6},{6,7},{7,8},{8,9},{9,10},{10,1... | collective-permute-start | bytes 786440 | tf_op jit(solution)/shard_map/ppermute | solution.py:11
  78.0 3.3 collective-permute-done
  81.3 4.4 collective-permute-start.1
  85.8 5.8 collective-permute-done.1
  91.7 1.9 collective-permute-start.2
  93.6 12.5 %collective-permute-done.2 = f32[256,256]{1,0:T(8,128)S(1)} collective-permute-done((f32[256,256]{1,0:T(8,128)S(1)}, f32[256,256]{1,0:T(8,128)S(1)}, u32[]{:S(2)}, u32[]{:S(2)}) %collective-permute-start.2) | collective-permute-done | bytes 262176 | tf_op jit(solution)/shard_map/ppermute | solution.py:11
  106.2 1.9 collective-permute-start.3
  108.1 12.1 %collective-permute-done.3 = f32[256,256]{1,0:T(8,128)S(1)} collective-permute-done((f32[256,256]{1,0:T(8,128)S(1)}, f32[256,256]{1,0:T(8,128)S(1)}, u32[]{:S(2)}, u32[]{:S(2)}) %collective-permute-start.3) | collective-permute-done | bytes 262176 | tf_op jit(solution)/shard_map/ppermute | solution.py:11
  120.3 1.9 collective-permute-start.4
  122.2 12.0 %collective-permute-done.4 = f32[256,256]{1,0:T(8,128)S(1)} collective-permute-done((f32[256,256]{1,0:T(8,128)S(1)}, f32[256,256]{1,0:T(8,128)S(1)}, u32[]{:S(2)}, u32[]{:S(2)}) %collective-permute-start.4) | collective-permute-done | bytes 262176 | tf_op jit(solution)/shard_map/ppermute | solution.py:11
  134.3 1.9 collective-permute-start.5
  136.3 12.0 %collective-permute-done.5 = f32[256,256]{1,0:T(8,128)S(1)} collective-permute-done((f32[256,256]{1,0:T(8,128)S(1)}, f32[256,256]{1,0:T(8,128)S(1)}, u32[]{:S(2)}, u32[]{:S(2)}) %collective-permute-start.5) | collective-permute-done | bytes 262176 | tf_op jit(solution)/shard_map/ppermute | solution.py:11
  148.3 1.9 collective-permute-start.6
  150.3 12.0 %collective-permute-done.6 = f32[256,256]{1,0:T(8,128)S(1)} collective-permute-done((f32[256,256]{1,0:T(8,128)S(1)}, f32[256,256]{1,0:T(8,128)S(1)}, u32[]{:S(2)}, u32[]{:S(2)}) %collective-permute-start.6) | collective-permute-done | bytes 262176 | tf_op jit(solution)/shard_map/ppermute | solution.py:11
  163.1 12.4 %collective-permute-start.7 = (bf16[256,256]{1,0:T(8,128)(2,1)S(1)}, bf16[256,256]{1,0:T(8,128)(2,1)S(1)}, u32[]{:S(2)}, u32[]{:S(2)}) collective-permute-start(bf16[256,256]{1,0:T(8,128)(2,1)S(1)} %get-tuple-element.13), channel_id=1, source_target_pairs={{0,95},{1,0},{2,1},{3,2},{4,3},{5,4},{6,5},{7,6},{8,7},{9,8},{10,9... | collective-permute-start | bytes 393224 | tf_op jit(solution)/shard_map/ppermute | solution.py:11
  176.5 3.4 collective-permute-start.8
  180.0 2.8 collective-permute-done.8
  182.8 7.7 collective-permute-start.9
  191.4 9.5 %collective-permute-start.10 = (bf16[256,256]{1,0:T(8,128)(2,1)S(1)}, bf16[256,256]{1,0:T(8,128)(2,1)S(1)}, u32[]{:S(2)}, u32[]{:S(2)}) collective-permute-start(bf16[256,256]{1,0:T(8,128)(2,1)S(1)} %collective-permute-done.9), channel_id=1, source_target_pairs={{0,95},{1,0},{2,1},{3,2},{4,3},{5,4},{6,5},{7,6},{8,7},{9,8},{10,9... | collective-permute-start | bytes 393224 | tf_op jit(solution)/shard_map/ppermute | solution.py:11
  201.9 9.5 %collective-permute-start.11 = (bf16[256,256]{1,0:T(8,128)(2,1)S(1)}, bf16[256,256]{1,0:T(8,128)(2,1)S(1)}, u32[]{:S(2)}, u32[]{:S(2)}) collective-permute-start(bf16[256,256]{1,0:T(8,128)(2,1)S(1)} %collective-permute-done.10), channel_id=1, source_target_pairs={{0,95},{1,0},{2,1},{3,2},{4,3},{5,4},{6,5},{7,6},{8,7},{9,8},{10,9... | collective-permute-start | bytes 393224 | tf_op jit(solution)/shard_map/ppermute | solution.py:11
  212.4 9.5 %collective-permute-start.12 = (bf16[256,256]{1,0:T(8,128)(2,1)S(1)}, bf16[256,256]{1,0:T(8,128)(2,1)S(1)}, u32[]{:S(2)}, u32[]{:S(2)}) collective-permute-start(bf16[256,256]{1,0:T(8,128)(2,1)S(1)} %collective-permute-done.11), channel_id=1, source_target_pairs={{0,95},{1,0},{2,1},{3,2},{4,3},{5,4},{6,5},{7,6},{8,7},{9,8},{10,9... | collective-permute-start | bytes 393224 | tf_op jit(solution)/shard_map/ppermute | solution.py:11
  222.9 9.7 %collective-permute-start.13 = (bf16[256,256]{1,0:T(8,128)(2,1)S(1)}, bf16[256,256]{1,0:T(8,128)(2,1)S(1)}, u32[]{:S(2)}, u32[]{:S(2)}) collective-permute-start(bf16[256,256]{1,0:T(8,128)(2,1)S(1)} %collective-permute-done.12), channel_id=1, source_target_pairs={{0,95},{1,0},{2,1},{3,2},{4,3},{5,4},{6,5},{7,6},{8,7},{9,8},{10,9... | collective-permute-start | bytes 393224 | tf_op jit(solution)/shard_map/ppermute | solution.py:11
  234.6 1.9 gather_fusion.1
  236.5 2.1 fusion.4
  238.6 3.4 copy.24
  242.4 2.5 copy.21
  245.1 119.3 %psum.15 = f32[256]{0:T(256)} all-reduce(f32[256]{0:T(256)S(1)} %get-tuple-element.12), channel_id=1, replica_groups=mesh['row'=8,'rep'=96] {'row','rep'}, use_global_device_ids=true, to_apply=%region_3.4 | all-reduce | flops 256 | bytes 2048 | tf_op jit(solution)/shard_map/psum | solution.py:63
  368.1 456.1 %all-reduce.2.cloned.1.call-done = f32[256,256]{0,1:T(8,128)} async-done(((f32[256,256]{0,1:T(8,128)}), f32[256,256]{0,1:T(8,128)}) %all-reduce.2.cloned.1.call-update) | async-done | bytes 262160 | tf_op jit(solution)/shard_map/psum | solution.py:63
  (64 shorter events, 17.7 us)
Async XLA Ops:
  7.2 55.5 %copy-start = (bf16[1,1,32,128,128]{4,3,2,1,0:T(8,128)(2,1)S(1)}, bf16[1,1,32,128,128]{4,3,2,1,0:T(8,128)(2,1)}, u32[]{:S(2)}) copy-start(bf16[1,1,32,128,128]{4,3,2,1,0:T(8,128)(2,1)} %param.11) | copy-start | bytes 3145732
  7.2 53.6 %all-gather.2.cloned.1.call-start = ((), (), s32[]{:S(2)}) async-start(), calls=%async_computation.1 | async-start | bytes 1179648 | tf_op jit(solution)/shard_map/all_gather | solution.py:33
  9.1 355.2 %reduce-scatter.2.cloned.1.call-start = ((), (), s32[]{:S(2)}) async-start(), calls=%async_computation.2 | async-start | bytes 2359296 | tf_op jit(solution)/shard_map/reduce_scatter | solution.py:54
  64.8 3.4 copy-start.6
  69.4 11.9 %collective-permute-start = (f32[256,256]{1,0:T(8,128)S(1)}, f32[256,256]{1,0:T(8,128)S(1)}, u32[]{:S(2)}, u32[]{:S(2)}) collective-permute-start(f32[256,256]{1,0:T(8,128)S(1)} %bitcast.81), channel_id=1, source_target_pairs={{0,1},{1,2},{2,3},{3,4},{4,5},{5,6},{6,7},{7,8},{8,9},{9,10},{10,1... | collective-permute-start | bytes 786440 | tf_op jit(solution)/shard_map/ppermute | solution.py:11
  81.3 10.3 %collective-permute-start.1 = (f32[256,256]{1,0:T(8,128)S(1)}, f32[256,256]{1,0:T(8,128)S(1)}, u32[]{:S(2)}, u32[]{:S(2)}) collective-permute-start(f32[256,256]{1,0:T(8,128)S(1)} %bitcast_add_fusion.6), channel_id=1, source_target_pairs={{0,1},{1,2},{2,3},{3,4},{4,5},{5,6},{6,7},{7,8},{8,9},{9,10},{10,1... | collective-permute-start | bytes 786440 | tf_op jit(solution)/shard_map/ppermute | solution.py:11
  91.7 14.5 %collective-permute-start.2 = (f32[256,256]{1,0:T(8,128)S(1)}, f32[256,256]{1,0:T(8,128)S(1)}, u32[]{:S(2)}, u32[]{:S(2)}) collective-permute-start(f32[256,256]{1,0:T(8,128)S(1)} %bitcast_add_fusion.5), channel_id=1, source_target_pairs={{0,1},{1,2},{2,3},{3,4},{4,5},{5,6},{6,7},{7,8},{8,9},{9,10},{10,1... | collective-permute-start | bytes 786440 | tf_op jit(solution)/shard_map/ppermute | solution.py:11
  106.2 14.1 %collective-permute-start.3 = (f32[256,256]{1,0:T(8,128)S(1)}, f32[256,256]{1,0:T(8,128)S(1)}, u32[]{:S(2)}, u32[]{:S(2)}) collective-permute-start(f32[256,256]{1,0:T(8,128)S(1)} %bitcast_add_fusion.4), channel_id=1, source_target_pairs={{0,1},{1,2},{2,3},{3,4},{4,5},{5,6},{6,7},{7,8},{8,9},{9,10},{10,1... | collective-permute-start | bytes 786440 | tf_op jit(solution)/shard_map/ppermute | solution.py:11
  108.1 54.2 %copy-start.4 = (bf16[256,256]{1,0:T(8,128)(2,1)S(1)}, bf16[256,256]{1,0:T(8,128)(2,1)}, u32[]{:S(2)}) copy-start(bf16[256,256]{1,0:T(8,128)(2,1)} %param.15) | copy-start | bytes 393220
  108.1 54.2 %copy-start.5 = (f32[256]{0:T(256)S(1)}, f32[256]{0:T(256)}, u32[]{:S(2)}) copy-start(f32[256]{0:T(256)} %param.10) | copy-start | bytes 3076
  120.3 14.0 %collective-permute-start.4 = (f32[256,256]{1,0:T(8,128)S(1)}, f32[256,256]{1,0:T(8,128)S(1)}, u32[]{:S(2)}, u32[]{:S(2)}) collective-permute-start(f32[256,256]{1,0:T(8,128)S(1)} %bitcast_add_fusion.3), channel_id=1, source_target_pairs={{0,1},{1,2},{2,3},{3,4},{4,5},{5,6},{6,7},{7,8},{8,9},{9,10},{10,1... | collective-permute-start | bytes 786440 | tf_op jit(solution)/shard_map/ppermute | solution.py:11
  134.3 14.0 %collective-permute-start.5 = (f32[256,256]{1,0:T(8,128)S(1)}, f32[256,256]{1,0:T(8,128)S(1)}, u32[]{:S(2)}, u32[]{:S(2)}) collective-permute-start(f32[256,256]{1,0:T(8,128)S(1)} %bitcast_add_fusion.2), channel_id=1, source_target_pairs={{0,1},{1,2},{2,3},{3,4},{4,5},{5,6},{6,7},{7,8},{8,9},{9,10},{10,1... | collective-permute-start | bytes 786440 | tf_op jit(solution)/shard_map/ppermute | solution.py:11
  148.3 13.9 %collective-permute-start.6 = (f32[256,256]{1,0:T(8,128)S(1)}, f32[256,256]{1,0:T(8,128)S(1)}, u32[]{:S(2)}, u32[]{:S(2)}) collective-permute-start(f32[256,256]{1,0:T(8,128)S(1)} %bitcast_add_fusion.1), channel_id=1, source_target_pairs={{0,1},{1,2},{2,3},{3,4},{4,5},{5,6},{6,7},{7,8},{8,9},{9,10},{10,1... | collective-permute-start | bytes 786440 | tf_op jit(solution)/shard_map/ppermute | solution.py:11
  163.1 13.4 %collective-permute-start.7 = (bf16[256,256]{1,0:T(8,128)(2,1)S(1)}, bf16[256,256]{1,0:T(8,128)(2,1)S(1)}, u32[]{:S(2)}, u32[]{:S(2)}) collective-permute-start(bf16[256,256]{1,0:T(8,128)(2,1)S(1)} %get-tuple-element.13), channel_id=1, source_target_pairs={{0,95},{1,0},{2,1},{3,2},{4,3},{5,4},{6,5},{7,6},{8,7},{9,8},{10,9... | collective-permute-start | bytes 393224 | tf_op jit(solution)/shard_map/ppermute | solution.py:11
  176.5 6.3 collective-permute-start.8
  182.8 8.6 %collective-permute-start.9 = (bf16[256,256]{1,0:T(8,128)(2,1)S(1)}, bf16[256,256]{1,0:T(8,128)(2,1)S(1)}, u32[]{:S(2)}, u32[]{:S(2)}) collective-permute-start(bf16[256,256]{1,0:T(8,128)(2,1)S(1)} %collective-permute-done.8), channel_id=1, source_target_pairs={{0,95},{1,0},{2,1},{3,2},{4,3},{5,4},{6,5},{7,6},{8,7},{9,8},{10,9... | collective-permute-start | bytes 393224 | tf_op jit(solution)/shard_map/ppermute | solution.py:11
  191.4 10.5 %collective-permute-start.10 = (bf16[256,256]{1,0:T(8,128)(2,1)S(1)}, bf16[256,256]{1,0:T(8,128)(2,1)S(1)}, u32[]{:S(2)}, u32[]{:S(2)}) collective-permute-start(bf16[256,256]{1,0:T(8,128)(2,1)S(1)} %collective-permute-done.9), channel_id=1, source_target_pairs={{0,95},{1,0},{2,1},{3,2},{4,3},{5,4},{6,5},{7,6},{8,7},{9,8},{10,9... | collective-permute-start | bytes 393224 | tf_op jit(solution)/shard_map/ppermute | solution.py:11
  201.9 10.5 %collective-permute-start.11 = (bf16[256,256]{1,0:T(8,128)(2,1)S(1)}, bf16[256,256]{1,0:T(8,128)(2,1)S(1)}, u32[]{:S(2)}, u32[]{:S(2)}) collective-permute-start(bf16[256,256]{1,0:T(8,128)(2,1)S(1)} %collective-permute-done.10), channel_id=1, source_target_pairs={{0,95},{1,0},{2,1},{3,2},{4,3},{5,4},{6,5},{7,6},{8,7},{9,8},{10,9... | collective-permute-start | bytes 393224 | tf_op jit(solution)/shard_map/ppermute | solution.py:11
  212.4 10.5 %collective-permute-start.12 = (bf16[256,256]{1,0:T(8,128)(2,1)S(1)}, bf16[256,256]{1,0:T(8,128)(2,1)S(1)}, u32[]{:S(2)}, u32[]{:S(2)}) collective-permute-start(bf16[256,256]{1,0:T(8,128)(2,1)S(1)} %collective-permute-done.11), channel_id=1, source_target_pairs={{0,95},{1,0},{2,1},{3,2},{4,3},{5,4},{6,5},{7,6},{8,7},{9,8},{10,9... | collective-permute-start | bytes 393224 | tf_op jit(solution)/shard_map/ppermute | solution.py:11
  222.9 10.7 %collective-permute-start.13 = (bf16[256,256]{1,0:T(8,128)(2,1)S(1)}, bf16[256,256]{1,0:T(8,128)(2,1)S(1)}, u32[]{:S(2)}, u32[]{:S(2)}) collective-permute-start(bf16[256,256]{1,0:T(8,128)(2,1)S(1)} %collective-permute-done.12), channel_id=1, source_target_pairs={{0,95},{1,0},{2,1},{3,2},{4,3},{5,4},{6,5},{7,6},{8,7},{9,8},{10,9... | collective-permute-start | bytes 393224 | tf_op jit(solution)/shard_map/ppermute | solution.py:11
  233.6 1.0 copy-start.1
  238.6 3.4 copy-start.7
  245.0 119.4 %copy-start.2 = (bf16[256,256]{1,0:T(8,128)(2,1)S(1)}, bf16[256,256]{1,0:T(8,128)(2,1)}, u32[]{:S(2)}) copy-start(bf16[256,256]{1,0:T(8,128)(2,1)} %param.8) | copy-start | bytes 393220
  245.0 121.3 %copy-start.3 = (bf16[256,256]{1,0:T(8,128)(2,1)S(1)}, bf16[256,256]{1,0:T(8,128)(2,1)}, u32[]{:S(2)}) copy-start(bf16[256,256]{1,0:T(8,128)(2,1)} %param.9) | copy-start | bytes 393220
  245.0 579.2 %all-reduce.2.cloned.1.call-start = ((), (), s32[]{:S(2)}) async-start(), calls=%async_computation.3 | async-start | bytes 524288 | tf_op jit(solution)/shard_map/psum | solution.py:63
Sparse Core Ops, SparseCore 0:
  11.0 49.7 all-gather.1
  245.1 49.5 reduce-scatter.1
  366.4 457.7 all-reduce.1
where the time goes:
time: 834 us; the launch traced here: 833 us
  waiting for transfers between devices  585 us (70%)
  blocking collectives  119 us (14%)
  starting transfers between devices  84.5 us (10%)
  local copies, waits for them, and re-layouts  16.9 us (2%)
  between operations  14.8 us (2%)
  matrix products  10.7 us (1%)
    psum x1, waiting for transfers between devices, shards(): lax.psum((local_weight, local_bias), ('row', 'rep'))  456 us
    psum x1, blocking collectives, shards(): lax.psum((local_weight, local_bias), ('row', 'rep'))  119 us
    ppermute x14, starting transfers between devices, passed_along(): lax.ppermute(shard, axis, [(i, (i + by) % size) for i in range(size)])  84.4 us
    ppermute x14, waiting for transfers between devices, passed_along(): lax.ppermute(shard, axis, [(i, (i + by) % size) for i in range(size)])  78.2 us
    all_gather x1, waiting for transfers between devices, shards(): gathered = lax.all_gather(xw, 'row', axis=0, tiled=True)  50.2 us
  transfers between devices with their start and end apart: 17, of which 16 were waited for; matrix products, arithmetic and copies ran while one was open for 0% of the time, Pallas kernels for 0%

commit v1 on v0

v1 whole, which is shorter than its diff:
```python
import jax
import jax.numpy as jnp
from jax import lax
from jax.experimental import pallas as pl
from jax.experimental.pallas import tpu as pltpu
from jax.sharding import PartitionSpec as P

K = 8
BF = jnp.bfloat16
F32 = jnp.float32


def forward_tiles(rows, cols, count, vals, source, even, odd, acc):
    acc[...] = jnp.zeros_like(acc)
    live = count[0]
    for t in range(vals.shape[0]):
        product = jnp.dot(vals[t], source[cols[t]], preferred_element_type=F32)
        acc[rows[t]] += jnp.where(t < live, product, 0.0)
    tile = vals.shape[1]
    for o in range(K):
        for h in range(2):
            part = acc[2 * o + h].astype(BF)
            target = odd if o % 2 else even
            target[o // 2, h * tile : (h + 1) * tile, :] = part


def backward_tiles(rows, cols, count, vals, even, odd, out, acc):
    acc[...] = jnp.zeros_like(acc)
    live = count[0]
    for t in range(vals.shape[0]):
        row = rows[t]
        place = (row // 4) * 2 + row % 2
        reached = jnp.where(row % 4 >= 2, odd[place], even[place])
        product = lax.dot_general(
            vals[t], reached, (((0,), (0,)), ((), ())), preferred_element_type=F32
        )
        acc[cols[t]] += jnp.where(t < live, product, 0.0)
    out[...] = acc[...].astype(BF)


def tiles_call(kernel, rows, cols, count, vals, arrays, outs):
    slots, tile = vals.shape[0], vals.shape[1]
    width = arrays[0].shape[-1]
    smem = pl.BlockSpec(memory_space=pltpu.SMEM)
    vmem = pl.BlockSpec(memory_space=pltpu.VMEM)
    return pl.pallas_call(
        kernel,
        out_shape=outs,
        in_specs=[smem] * 3 + [vmem] * (1 + len(arrays)),
        out_specs=jax.tree.map(lambda _: vmem, outs),
        scratch_shapes=[pltpu.VMEM((2 * K, tile, width), F32)],
        compiler_params=pltpu.CompilerParams(vmem_limit_bytes=24 * 1024 * 1024),
        cost_estimate=pl.CostEstimate(
            flops=2 * slots * tile * tile * width, bytes_accessed=3 << 20, transcendentals=0
        ),
    )(rows, cols, count, vals, *arrays)


def passed(shard, axis, to):
    size = lax.axis_size(axis)
    pairs = [(i, to(i)) for i in range(size)]
    return lax.ppermute(shard, axis, [(i, j % size) for i, j in pairs if j is not None])


def gathered(shard, axis, groups=None):
    size = lax.axis_size(axis) if groups is None else len(groups[0])
    copies = jnp.broadcast_to(shard[None], (size,) + shard.shape)
    return lax.all_to_all(copies, axis, 0, 0, axis_index_groups=groups)


def total_over_mesh(local_weight, local_bias, z_chips):
    reps = lax.axis_size("rep")
    rows = lax.axis_size("row")
    width = local_weight.shape[1]
    core = lax.axis_index("rep") % 2
    half = local_weight.shape[0] // 2
    piece = half // rows
    give = jnp.where(core == 0, local_weight[half:], local_weight[:half])
    keep = jnp.where(core == 0, local_weight[:half], local_weight[half:])
    bias = jnp.broadcast_to(local_bias[None, None], (rows, 1, width))
    pad = jnp.zeros((rows, 15, width), BF)

    weight = keep + passed(give, "rep", lambda i: i ^ 1).astype(F32)
    parts = jnp.concatenate(
        [weight.reshape(rows, piece, width).astype(BF), bias.astype(BF), pad], axis=1
    )
    summed = jnp.sum(lax.all_to_all(parts, "row", 0, 0).astype(F32), axis=0).astype(BF)
    line = [
        [y * 2 * z_chips + 2 * z + c for z in range(z_chips)]
        for y in range(reps // (2 * z_chips))
        for c in range(2)
    ]
    summed = jnp.sum(gathered(summed, "rep", line).astype(F32), axis=0).astype(BF)
    across = [
        [y * 2 * z_chips + i for y in range(reps // (2 * z_chips))] for i in range(2 * z_chips)
    ]
    summed = jnp.sum(gathered(summed, "rep", across).astype(F32), axis=0)
    other = passed(summed, "rep", lambda i: i ^ 1)
    low = jnp.where(core == 0, summed, other)
    high = jnp.where(core == 0, other, summed)
    bias_sum = (low + high)[piece]
    both = jnp.stack([low[:piece], high[:piece]])
    everything = gathered(both, "row")
    weight_sum = jnp.swapaxes(everything, 0, 1).reshape(2 * half, width)
    return weight_sum, bias_sum


def shards(features, weight, bias, tile_vals, tile_rows, tile_cols, tile_counts, grad_out):
    block, width = features.shape
    vals = tile_vals[0, 0]
    rows = tile_rows[0, 0]
    cols = tile_cols[0, 0]
    count = tile_counts[0]
    tile = vals.shape[1]
    group_rows = lax.axis_size("row")
    core = lax.axis_index("rep") % 2
    wide = jax.ShapeDtypeStruct((K // 2, block, width), BF)

    with jax.named_scope("gather_features"):
        source = gathered(features, "row").reshape(group_rows * block // tile, tile, width)
    with jax.named_scope("forward_tiles"):
        even, odd = tiles_call(
            forward_tiles, rows, cols, count, vals, [source], (wide, wide)
        )
    with jax.named_scope("window_sum"):
        far = passed(odd[3], "rep", lambda i: i + 7 if i % 2 else None)
        other = passed(odd, "rep", lambda i: i ^ 1)
        shifted = jnp.concatenate([jnp.zeros_like(other[:1]), other[:3]])
        sums = even.astype(F32) + jnp.where(core == 0, shifted, other).astype(F32)
        near = passed(jnp.stack([sums[1], sums[3]]).astype(BF), "rep", lambda i: i + 2)
        middle = passed((sums[2] + near[1].astype(F32)).astype(BF), "rep", lambda i: i + 4)
        aggregate = sums[0] + near[0].astype(F32) + far.astype(F32) + middle.astype(F32)
    with jax.named_scope("pointwise"):
        top = aggregate.astype(BF)
        rest = (aggregate - top.astype(F32)).astype(BF)
        pre = (
            jnp.dot(top, weight, preferred_element_type=F32)
            + jnp.dot(rest, weight, preferred_element_type=F32)
            + bias[None, :]
        )
        activations = jax.nn.silu(pre).astype(BF)
        sig = jax.nn.sigmoid(pre)
        grad_pre = (grad_out.astype(F32) * sig * (1.0 + pre * (1.0 - sig))).astype(BF)
        local_weight = lax.dot_general(
            top, grad_pre, (((0,), (0,)), ((), ())), preferred_element_type=F32
        )
        local_bias = jnp.sum(grad_pre.astype(F32), axis=0)
    with jax.named_scope("window_gather"):
        far = passed(grad_pre, "rep", lambda i: i - 7 if i % 2 == 0 else None)
        second = passed(grad_pre, "rep", lambda i: i - 4)
        near = passed(jnp.stack([grad_pre, second]), "rep", lambda i: i - 2)
        mine = jnp.stack([grad_pre, near[0], second, near[1]])
        ahead = jnp.stack([near[0], second, near[1], near[1]])
        other = passed(jnp.where(core == 0, ahead, mine), "rep", lambda i: i ^ 1)
        last = jnp.where(core == 0, other[3], far)
        other = jnp.concatenate([other[:3], last[None]])
    with jax.named_scope("backward_tiles"):
        terms = tiles_call(
            backward_tiles,
            rows,
            cols,
            count,
            vals,
            [mine.reshape(K, tile, width), other.reshape(K, tile, width)],
            jax.ShapeDtypeStruct((group_rows * block // tile, tile, width), BF),
        ).reshape(group_rows, block, width)
    with jax.named_scope("source_sum"):
        arrived = lax.all_to_all(terms, "row", 0, 0)
        source_grad = jnp.sum(arrived.astype(F32), axis=0).astype(BF)
        grad_features = lax.dot_general(
            source_grad, weight, (((1,), (1,)), ((), ())), preferred_element_type=F32
        ).astype(BF)
    with jax.named_scope("weight_sum"):
        grad_weight, grad_bias = total_over_mesh(local_weight, local_bias, 12)
    return (activations, grad_features, grad_weight, grad_bias)


def solution(mesh):
    placed = (
        P(("row", "rep"), None),
        P(),
        P(),
        P("row", "rep", None, None, None),
        P("row", "rep", None),
        P("row", "rep", None),
        P("row", "rep"),
        P(("row", "rep"), None),
    )
    return jax.shard_map(
        shards,
        mesh=mesh,
        in_specs=placed,
        out_specs=(P(("row", "rep"), None), P(("row", "rep"), None), P(), P()),
        check_vma=False,
    )
```

time: 834 us -> 166 us (0.20)
  waiting for transfers between devices: 585 us -> 66.1 us
  blocking collectives: 119 us -> 8.18 us
  between operations: 14.8 us -> 1.65 us
  local copies, waits for them, and re-layouts: 16.9 us -> 6.14 us
  starting transfers between devices: 84.5 us -> 75 us
  matrix products: 10.7 us -> 2.19 us
    psum x1 -> x0, waiting for transfers between devices: 456 us -> none  [shards(): lax.psum((local_weight, local_bias), ('row', 'rep'))]
    psum x1 -> x0, blocking collectives: 119 us -> none  [shards(): lax.psum((local_weight, local_bias), ('row', 'rep'))]
    all_gather x1 -> x0, waiting for transfers between devices: 50.2 us -> none  [shards(): gathered = lax.all_gather(xw, 'row', axis=0, tiled=True)]
    ppermute x14 -> x10, waiting for transfers between devices: 78.2 us -> 36.8 us  [passed(): lax.ppermute(shard, axis, [(i, j % size) for i, j in pairs if j is not No...]
    ppermute x14 -> x10, starting transfers between devices: 84.4 us -> 54.6 us  [passed(): lax.ppermute(shard, axis, [(i, j % size) for i, j in pairs if j is not No...]
    all_to_all x0 -> x5, waiting for transfers between devices: none -> 29.2 us  [the longest x4 16.9 us: gathered(): return lax.all_to_all(copies, axis, 0, 0, axis_index_groups=groups)]
    all_to_all x0 -> x5, starting transfers between devices: none -> 20.5 us  [the longest x4 16.7 us: gathered(): return lax.all_to_all(copies, axis, 0, 0, axis_index_groups=groups)]
    dot_general x3 -> x0, local copies, waits for them, and re-layouts: 9.37 us -> none  [the longest x1 3.41 us: shards(): jnp.einsum('tij,tjh->tih', vals, source, preferred_element_type=jnp.float32)]
  transfers between devices with their start and end apart: 17 -> 15, of which waited for: 16 -> 10; matrix products, arithmetic and copies ran while one was open for 0% -> 2% of each run, Pallas kernels for 0% -> 2%
where the time goes in v1:
time: 166 us; the launch traced here: 165 us
  starting transfers between devices  75 us (45%)
  waiting for transfers between devices  66.1 us (40%)
  blocking collectives  8.18 us (5%)
  local copies, waits for them, and re-layouts  6.14 us (4%)
  Pallas kernels  4.07 us (2%)
  matrix products  2.19 us (1%)
    ppermute x10, starting transfers between devices, passed(): lax.ppermute(shard, axis, [(i, j % size) for i, j in pairs if j is not No...  54.6 us
    ppermute x10, waiting for transfers between devices, passed(): lax.ppermute(shard, axis, [(i, j % size) for i, j in pairs if j is not No...  36.8 us
    all_to_all x4, waiting for transfers between devices, gathered(): return lax.all_to_all(copies, axis, 0, 0, axis_index_groups=groups)  16.9 us
    all_to_all x4, starting transfers between devices, gathered(): return lax.all_to_all(copies, axis, 0, 0, axis_index_groups=groups)  16.7 us
    all_to_all x1, waiting for transfers between devices, shards(): arrived = lax.all_to_all(terms, 'row', 0, 0)  12.3 us
    all_to_all x1, blocking collectives, total_over_mesh(): lax.all_to_all(parts, 'row', 0, 0).astype(F32)  8.18 us
    pallas_call x2, Pallas kernels, tiles_call(): pl.pallas_call(kernel, out_shape=outs, in_specs=[smem] * 3 + [vmem] * (1...  4.07 us
    broadcast_in_dim x4, local copies, waits for them, and re-layouts, gathered(): copies = jnp.broadcast_to(shard[None], (size,) + shard.shape)  4.06 us
  transfers between devices with their start and end apart: 15, of which 10 were waited for; matrix products, arithmetic and copies ran while one was open for 2% of the time, Pallas kernels for 2%

profile of v1, /device:TPU:1, one launch (start us, length us, event | category | flops | bytes accessed | tf_op | source)
XLA Modules:
  0.0 164.9 jit_solution(12433034499470977589)
XLA Ops:
  0.6 2.0 %broadcast_in_dim.14 = bf16[8,256,256]{2,1,0:T(8,128)(2,1)} broadcast(bf16[256,256]{1,0:T(8,128)(2,1)} %param.8), dimensions={1,2} | broadcast | bytes 1179648 | tf_op jit(solution)/shard_map/gather_features/broadcast_in_dim | solution.py:67
  2.6 6.0 %all-to-all-start = ((bf16[8,256,256]{2,1,0:T(8,128)(2,1)}), bf16[8,256,256]{2,1,0:T(8,128)(2,1)S(1)}, u32[]{:S(2)}, u32[]{:S(2)}) async-start(bf16[8,256,256]{2,1,0:T(8,128)(2,1)} %broadcast_in_dim.14), calls=%async_computation | async-start | bytes 2097152 | tf_op jit(solution)/shard_map/gather_features/all_to_all | solution.py:68
  9.3 8.8 %all-to-all-done = bf16[8,256,256]{2,1,0:T(8,128)(2,1)S(1)} async-done(((bf16[8,256,256]{2,1,0:T(8,128)(2,1)}), bf16[8,256,256]{2,1,0:T(8,128)(2,1)S(1)}, u32[]{:S(2)}, u32[]{:S(2)}) %all-to-all-start) | async-done | bytes 1048608 | tf_op jit(solution)/shard_map/gather_features/all_to_all | solution.py:68
  18.8 1.5 forward_tiles.1
  20.2 11.2 %collective-permute-start = (bf16[4,256,256]{2,1,0:T(8,128)(2,1)S(1)}, bf16[4,256,256]{2,1,0:T(8,128)(2,1)S(1)}, u32[]{:S(2)}, u32[]{:S(2)}) collective-permute-start(bf16[4,256,256]{2,1,0:T(8,128)(2,1)S(1)} %get-tuple-element.7), channel_id=1, source_target_pairs={{0,1},{1,0},{2,3},{3,2},{4,5},{5,4},{6,7},{7,6},{8,9},{9,8},{10,11... | collective-permute-start | bytes 1572872 | tf_op jit(solution)/shard_map/window_sum/ppermute | solution.py:62
  31.4 1.5 collective-permute-done
  33.2 1.9 %collective-permute-start.1 = (bf16[2,256,256]{2,1,0:T(8,128)(2,1)S(1)}, bf16[2,256,256]{2,1,0:T(8,128)(2,1)S(1)}, u32[]{:S(2)}, u32[]{:S(2)}) collective-permute-start(bf16[2,256,256]{2,1,0:T(8,128)(2,1)S(1)} %pad_maximum_fusion.3), channel_id=1, source_target_pairs={{0,2},{1,3},{2,4},{3,5},{4,6},{5,7},{6,8},{7,9},{8,10},{9,11},{10,... | collective-permute-start | bytes 786440 | tf_op jit(solution)/shard_map/window_sum/ppermute | solution.py:62
  35.2 10.3 %collective-permute-start.2 = (bf16[256,256]{1,0:T(8,128)(2,1)S(1)}, bf16[256,256]{1,0:T(8,128)(2,1)S(1)}, u32[]{:S(2)}, u32[]{:S(2)}) collective-permute-start(bf16[256,256]{1,0:T(8,128)(2,1)S(1)} %slice_bitcast_fusion.1), channel_id=1, source_target_pairs={{1,8},{3,10},{5,12},{7,14},{9,16},{11,18},{13,20},{15,22},{17,24},... | collective-permute-start | bytes 393224 | tf_op jit(solution)/shard_map/window_sum/ppermute | solution.py:62
  45.5 15.7 %collective-permute-done.1 = bf16[2,256,256]{2,1,0:T(8,128)(2,1)S(1)} collective-permute-done((bf16[2,256,256]{2,1,0:T(8,128)(2,1)S(1)}, bf16[2,256,256]{2,1,0:T(8,128)(2,1)S(1)}, u32[]{:S(2)}, u32[]{:S(2)}) %collective-permute-start.1) | collective-permute-done | bytes 262176 | tf_op jit(solution)/shard_map/window_sum/ppermute | solution.py:62
  61.2 1.9 %collective-permute-start.3 = (bf16[256,256]{1,0:T(8,128)(2,1)S(1)}, bf16[256,256]{1,0:T(8,128)(2,1)S(1)}, u32[]{:S(2)}, u32[]{:S(2)}) collective-permute-start(bf16[256,256]{1,0:T(8,128)(2,1)S(1)} %fusion.7), channel_id=1, source_target_pairs={{0,4},{1,5},{2,6},{3,7},{4,8},{5,9},{6,10},{7,11},{8,12},{9,13},{1... | collective-permute-start | bytes 393224 | tf_op jit(solution)/shard_map/window_sum/ppermute | solution.py:62
  63.1 10.2 %collective-permute-done.3 = bf16[256,256]{1,0:T(8,128)(2,1)S(1)} collective-permute-done((bf16[256,256]{1,0:T(8,128)(2,1)S(1)}, bf16[256,256]{1,0:T(8,128)(2,1)S(1)}, u32[]{:S(2)}, u32[]{:S(2)}) %collective-permute-start.3) | collective-permute-done | bytes 131104 | tf_op jit(solution)/shard_map/window_sum/ppermute | solution.py:62
  74.1 0.9 multiply_convert_fusion.1
  75.4 5.5 %collective-permute-start.8 = (f32[128,256]{1,0:T(8,128)S(1)}, f32[128,256]{1,0:T(8,128)S(1)}, u32[]{:S(2)}, u32[]{:S(2)}) collective-permute-start(f32[128,256]{1,0:T(8,128)S(1)} %slice_select_fusion), channel_id=1, source_target_pairs={{0,1},{1,0},{2,3},{3,2},{4,5},{5,4},{6,7},{7,6},{8,9},{9,8},{10,11... | collective-permute-start | bytes 393224 | tf_op jit(solution)/shard_map/weight_sum/ppermute | solution.py:62
  81.0 0.9 collective-permute-done.8
  82.0 8.2 %all_to_all.30 = bf16[8,32,256]{2,1,0:T(8,128)(2,1)S(1)} all-to-all(bf16[8,32,256]{2,1,0:T(8,128)(2,1)S(1)} %maximum_maximum_fusion), channel_id=1, replica_groups=mesh['row'=8,'rep'=96] {'row'}, dimensions={0} | all-to-all | bytes 262144 | tf_op jit(solution)/shard_map/weight_sum/all_to_all | solution.py:87
  90.9 3.5 %all-to-all-start.3 = ((bf16[12,32,256]{2,1,0:T(8,128)(2,1)}), bf16[12,32,256]{2,1,0:T(8,128)(2,1)S(1)}, u32[]{:S(2)}, u32[]{:S(2)}) async-start(bf16[12,32,256]{2,1,0:T(8,128)(2,1)} %broadcast_in_dim.18), calls=%async_computation.3 | async-start | bytes 393216 | tf_op jit(solution)/shard_map/weight_sum/all_to_all | solution.py:68
  94.4 5.9 %collective-permute-start.4 = (bf16[256,256]{1,0:T(8,128)(2,1)S(1)}, bf16[256,256]{1,0:T(8,128)(2,1)S(1)}, u32[]{:S(2)}, u32[]{:S(2)}) collective-permute-start(bf16[256,256]{1,0:T(8,128)(2,1)S(1)} %get-tuple-element.9), channel_id=1, source_target_pairs={{0,92},{1,93},{2,94},{3,95},{4,0},{5,1},{6,2},{7,3},{8,4},{9,5},{1... | collective-permute-start | bytes 393224 | tf_op jit(solution)/shard_map/window_gather/ppermute | solution.py:62
  100.3 6.3 %collective-permute-done.4 = bf16[256,256]{1,0:T(8,128)(2,1)S(1)} collective-permute-done((bf16[256,256]{1,0:T(8,128)(2,1)S(1)}, bf16[256,256]{1,0:T(8,128)(2,1)S(1)}, u32[]{:S(2)}, u32[]{:S(2)}) %collective-permute-start.4) | collective-permute-done | bytes 131104 | tf_op jit(solution)/shard_map/window_gather/ppermute | solution.py:62
  106.7 8.6 %collective-permute-start.5 = (bf16[2,256,256]{2,1,0:T(8,128)(2,1)S(1)}, bf16[2,256,256]{2,1,0:T(8,128)(2,1)S(1)}, u32[]{:S(2)}, u32[]{:S(2)}) collective-permute-start(bf16[2,256,256]{2,1,0:T(8,128)(2,1)S(1)} %pad_maximum_fusion.4), channel_id=1, source_target_pairs={{0,94},{1,95},{2,0},{3,1},{4,2},{5,3},{6,4},{7,5},{8,6},{9,7},{10,... | collective-permute-start | bytes 786440 | tf_op jit(solution)/shard_map/window_gather/ppermute | solution.py:62
  115.3 1.3 collective-permute-start.7
  117.3 3.7 %all-to-all-start.4 = ((bf16[4,32,256]{2,1,0:T(8,128)(2,1)}), bf16[4,32,256]{2,1,0:T(8,128)(2,1)S(1)}, u32[]{:S(2)}, u32[]{:S(2)}) async-start(bf16[4,32,256]{2,1,0:T(8,128)(2,1)} %broadcast_in_dim.19), calls=%async_computation.4 | async-start | bytes 131072 | tf_op jit(solution)/shard_map/weight_sum/all_to_all | solution.py:68
  121.0 2.2 %collective-permute-done.5 = bf16[2,256,256]{2,1,0:T(8,128)(2,1)S(1)} collective-permute-done((bf16[2,256,256]{2,1,0:T(8,128)(2,1)S(1)}, bf16[2,256,256]{2,1,0:T(8,128)(2,1)S(1)}, u32[]{:S(2)}, u32[]{:S(2)}) %collective-permute-start.5) | collective-permute-done | bytes 262176 | tf_op jit(solution)/shard_map/window_gather/ppermute | solution.py:62
  123.2 4.8 %all-to-all-done.4 = bf16[4,32,256]{2,1,0:T(8,128)(2,1)S(1)} async-done(((bf16[4,32,256]{2,1,0:T(8,128)(2,1)}), bf16[4,32,256]{2,1,0:T(8,128)(2,1)S(1)}, u32[]{:S(2)}, u32[]{:S(2)}) %all-to-all-start.4) | async-done | bytes 65568 | tf_op jit(solution)/shard_map/weight_sum/all_to_all | solution.py:68
  128.1 6.1 %collective-permute-start.9 = (f32[32,256]{1,0:T(8,128)S(1)}, f32[32,256]{1,0:T(8,128)S(1)}, u32[]{:S(2)}, u32[]{:S(2)}) collective-permute-start(f32[32,256]{1,0:T(8,128)S(1)} %convert_reduce_fusion), channel_id=1, source_target_pairs={{0,1},{1,0},{2,3},{3,2},{4,5},{5,4},{6,7},{7,6},{8,9},{9,8},{10,11... | collective-permute-start | bytes 98312 | tf_op jit(solution)/shard_map/weight_sum/ppermute | solution.py:62
  134.3 1.9 %collective-permute-start.6 = (bf16[4,256,256]{2,1,0:T(8,128)(2,1)S(1)}, bf16[4,256,256]{2,1,0:T(8,128)(2,1)S(1)}, u32[]{:S(2)}, u32[]{:S(2)}) collective-permute-start(bf16[4,256,256]{2,1,0:T(8,128)(2,1)S(1)} %get-tuple-element.12), channel_id=1, source_target_pairs={{0,1},{1,0},{2,3},{3,2},{4,5},{5,4},{6,7},{7,6},{8,9},{9,8},{10,11... | collective-permute-start | bytes 1572872 | tf_op jit(solution)/shard_map/window_gather/ppermute | solution.py:62
  136.3 0.7 broadcast_in_dim.20
  137.0 3.4 %all-to-all-start.5 = ((f32[8,2,16,256]{3,2,1,0:T(8,128)}), f32[8,2,16,256]{3,2,1,0:T(8,128)S(1)}, u32[]{:S(2)}, u32[]{:S(2)}) async-start(f32[8,2,16,256]{3,2,1,0:T(8,128)} %broadcast_in_dim.20), calls=%async_computation.5 | async-start | bytes 524288 | tf_op jit(solution)/shard_map/weight_sum/all_to_all | solution.py:68
  140.5 2.6 %backward_tiles.1 = bf16[16,128,256]{2,1,0:T(8,128)(2,1)} custom-call(s32[32]{0:T(128)S(1)} %bitcast.50, s32[32]{0:T(128)S(1)} %bitcast.52, s32[1]{0:T(128)} %bitcast.43.count, bf16[32,128,128]{2,1,0:T(8,128)(2,1)S(1)} %bitcast.45, bf16[8,128,256]{2,1,0:T(8,128)(2,1)S(1)} %bitcast.47, bf16[8,128,256]{2,1,0:T(8,128)(2,1)S(1)} %bitcast.48), custom_call_target="tpu_custom_call" | custom-call | flops 268435456 | bytes 3145728 | tf_op jit(solution)/shard_map/backward_tiles/pallas_call | solution.py:46
  143.2 3.3 %all-to-all-done.5 = f32[8,2,16,256]{3,2,1,0:T(8,128)S(1)} async-done(((f32[8,2,16,256]{3,2,1,0:T(8,128)}), f32[8,2,16,256]{3,2,1,0:T(8,128)S(1)}, u32[]{:S(2)}, u32[]{:S(2)}) %all-to-all-start.5) | async-done | bytes 262176 | tf_op jit(solution)/shard_map/weight_sum/all_to_all | solution.py:68
  146.5 3.8 %all-to-all-start.1 = ((bf16[8,256,256]{2,1,0:T(8,128)(2,1)}), bf16[8,256,256]{2,1,0:T(8,128)(2,1)S(1)}, u32[]{:S(2)}, u32[]{:S(2)}) async-start(bf16[8,256,256]{2,1,0:T(8,128)(2,1)} %bitcast.14), calls=%async_computation.1 | async-start | bytes 2097152 | tf_op jit(solution)/shard_map/source_sum/all_to_all | solution.py:168
  151.6 12.3 %all-to-all-done.1 = bf16[8,256,256]{2,1,0:T(8,128)(2,1)S(1)} async-done(((bf16[8,256,256]{2,1,0:T(8,128)(2,1)}), bf16[8,256,256]{2,1,0:T(8,128)(2,1)S(1)}, u32[]{:S(2)}, u32[]{:S(2)}) %all-to-all-start.1) | async-done | bytes 1048608 | tf_op jit(solution)/shard_map/source_sum/all_to_all | solution.py:168
  164.0 0.9 convolution_convert_fusion
  (50 shorter events, 5.4 us)
Async XLA Ops:
  0.6 72.8 %copy-start = (bf16[256,256]{1,0:T(8,128)(2,1)S(1)}, bf16[256,256]{1,0:T(8,128)(2,1)}, u32[]{:S(2)}) copy-start(bf16[256,256]{1,0:T(8,128)(2,1)} %param.9) | copy-start | bytes 393220
  2.6 15.5 %copy-start.1 = (bf16[1,1,32,128,128]{4,3,2,1,0:T(8,128)(2,1)S(1)}, bf16[1,1,32,128,128]{4,3,2,1,0:T(8,128)(2,1)}, u32[]{:S(2)}) copy-start(bf16[1,1,32,128,128]{4,3,2,1,0:T(8,128)(2,1)} %param.11) | copy-start | bytes 3145732
  2.6 15.4 %all-to-all-start = ((bf16[8,256,256]{2,1,0:T(8,128)(2,1)}), bf16[8,256,256]{2,1,0:T(8,128)(2,1)S(1)}, u32[]{:S(2)}, u32[]{:S(2)}) async-start(bf16[8,256,256]{2,1,0:T(8,128)(2,1)} %broadcast_in_dim.14), calls=%async_computation | async-start | bytes 2097152 | tf_op jit(solution)/shard_map/gather_features/all_to_all | solution.py:68
  18.1 0.7 copy-start.2
  18.1 0.7 copy-start.3
  20.2 12.7 %collective-permute-start = (bf16[4,256,256]{2,1,0:T(8,128)(2,1)S(1)}, bf16[4,256,256]{2,1,0:T(8,128)(2,1)S(1)}, u32[]{:S(2)}, u32[]{:S(2)}) collective-permute-start(bf16[4,256,256]{2,1,0:T(8,128)(2,1)S(1)} %get-tuple-element.7), channel_id=1, source_target_pairs={{0,1},{1,0},{2,3},{3,2},{4,5},{5,4},{6,7},{7,6},{8,9},{9,8},{10,11... | collective-permute-start | bytes 1572872 | tf_op jit(solution)/shard_map/window_sum/ppermute | solution.py:62
  33.2 27.9 %collective-permute-start.1 = (bf16[2,256,256]{2,1,0:T(8,128)(2,1)S(1)}, bf16[2,256,256]{2,1,0:T(8,128)(2,1)S(1)}, u32[]{:S(2)}, u32[]{:S(2)}) collective-permute-start(bf16[2,256,256]{2,1,0:T(8,128)(2,1)S(1)} %pad_maximum_fusion.3), channel_id=1, source_target_pairs={{0,2},{1,3},{2,4},{3,5},{4,6},{5,7},{6,8},{7,9},{8,10},{9,11},{10,... | collective-permute-start | bytes 786440 | tf_op jit(solution)/shard_map/window_sum/ppermute | solution.py:62
  35.2 27.9 %collective-permute-start.2 = (bf16[256,256]{1,0:T(8,128)(2,1)S(1)}, bf16[256,256]{1,0:T(8,128)(2,1)S(1)}, u32[]{:S(2)}, u32[]{:S(2)}) collective-permute-start(bf16[256,256]{1,0:T(8,128)(2,1)S(1)} %slice_bitcast_fusion.1), channel_id=1, source_target_pairs={{1,8},{3,10},{5,12},{7,14},{9,16},{11,18},{13,20},{15,22},{17,24},... | collective-permute-start | bytes 393224 | tf_op jit(solution)/shard_map/window_sum/ppermute | solution.py:62
  61.2 12.2 %collective-permute-start.3 = (bf16[256,256]{1,0:T(8,128)(2,1)S(1)}, bf16[256,256]{1,0:T(8,128)(2,1)S(1)}, u32[]{:S(2)}, u32[]{:S(2)}) collective-permute-start(bf16[256,256]{1,0:T(8,128)(2,1)S(1)} %fusion.7), channel_id=1, source_target_pairs={{0,4},{1,5},{2,6},{3,7},{4,8},{5,9},{6,10},{7,11},{8,12},{9,13},{1... | collective-permute-start | bytes 393224 | tf_op jit(solution)/shard_map/window_sum/ppermute | solution.py:62
  73.4 0.7 copy-start.5
  74.1 0.9 copy-start.4
  75.4 6.4 %collective-permute-start.8 = (f32[128,256]{1,0:T(8,128)S(1)}, f32[128,256]{1,0:T(8,128)S(1)}, u32[]{:S(2)}, u32[]{:S(2)}) collective-permute-start(f32[128,256]{1,0:T(8,128)S(1)} %slice_select_fusion), channel_id=1, source_target_pairs={{0,1},{1,0},{2,3},{3,2},{4,5},{5,4},{6,7},{7,6},{8,9},{9,8},{10,11... | collective-permute-start | bytes 393224 | tf_op jit(solution)/shard_map/weight_sum/ppermute | solution.py:62
  90.9 25.7 %all-to-all-start.3 = ((bf16[12,32,256]{2,1,0:T(8,128)(2,1)}), bf16[12,32,256]{2,1,0:T(8,128)(2,1)S(1)}, u32[]{:S(2)}, u32[]{:S(2)}) async-start(bf16[12,32,256]{2,1,0:T(8,128)(2,1)} %broadcast_in_dim.18), calls=%async_computation.3 | async-start | bytes 393216 | tf_op jit(solution)/shard_map/weight_sum/all_to_all | solution.py:68
  94.4 12.2 %collective-permute-start.4 = (bf16[256,256]{1,0:T(8,128)(2,1)S(1)}, bf16[256,256]{1,0:T(8,128)(2,1)S(1)}, u32[]{:S(2)}, u32[]{:S(2)}) collective-permute-start(bf16[256,256]{1,0:T(8,128)(2,1)S(1)} %get-tuple-element.9), channel_id=1, source_target_pairs={{0,92},{1,93},{2,94},{3,95},{4,0},{5,1},{6,2},{7,3},{8,4},{9,5},{1... | collective-permute-start | bytes 393224 | tf_op jit(solution)/shard_map/window_gather/ppermute | solution.py:62
  106.7 16.6 %collective-permute-start.5 = (bf16[2,256,256]{2,1,0:T(8,128)(2,1)S(1)}, bf16[2,256,256]{2,1,0:T(8,128)(2,1)S(1)}, u32[]{:S(2)}, u32[]{:S(2)}) collective-permute-start(bf16[2,256,256]{2,1,0:T(8,128)(2,1)S(1)} %pad_maximum_fusion.4), channel_id=1, source_target_pairs={{0,94},{1,95},{2,0},{3,1},{4,2},{5,3},{6,4},{7,5},{8,6},{9,7},{10,... | collective-permute-start | bytes 786440 | tf_op jit(solution)/shard_map/window_gather/ppermute | solution.py:62
  115.3 25.2 %collective-permute-start.7 = (bf16[256,256]{1,0:T(8,128)(2,1)S(1)}, bf16[256,256]{1,0:T(8,128)(2,1)S(1)}, u32[]{:S(2)}, u32[]{:S(2)}) collective-permute-start(bf16[256,256]{1,0:T(8,128)(2,1)S(1)} %get-tuple-element.9), channel_id=1, source_target_pairs={{0,89},{2,91},{4,93},{6,95},{8,1},{10,3},{12,5},{14,7},{16,9},{18,... | collective-permute-start | bytes 393224 | tf_op jit(solution)/shard_map/window_gather/ppermute | solution.py:62
  117.3 10.8 %all-to-all-start.4 = ((bf16[4,32,256]{2,1,0:T(8,128)(2,1)}), bf16[4,32,256]{2,1,0:T(8,128)(2,1)S(1)}, u32[]{:S(2)}, u32[]{:S(2)}) async-start(bf16[4,32,256]{2,1,0:T(8,128)(2,1)} %broadcast_in_dim.19), calls=%async_computation.4 | async-start | bytes 131072 | tf_op jit(solution)/shard_map/weight_sum/all_to_all | solution.py:68
  128.1 8.2 %collective-permute-start.9 = (f32[32,256]{1,0:T(8,128)S(1)}, f32[32,256]{1,0:T(8,128)S(1)}, u32[]{:S(2)}, u32[]{:S(2)}) collective-permute-start(f32[32,256]{1,0:T(8,128)S(1)} %convert_reduce_fusion), channel_id=1, source_target_pairs={{0,1},{1,0},{2,3},{3,2},{4,5},{5,4},{6,7},{7,6},{8,9},{9,8},{10,11... | collective-permute-start | bytes 98312 | tf_op jit(solution)/shard_map/weight_sum/ppermute | solution.py:62
  134.3 6.1 %collective-permute-start.6 = (bf16[4,256,256]{2,1,0:T(8,128)(2,1)S(1)}, bf16[4,256,256]{2,1,0:T(8,128)(2,1)S(1)}, u32[]{:S(2)}, u32[]{:S(2)}) collective-permute-start(bf16[4,256,256]{2,1,0:T(8,128)(2,1)S(1)} %get-tuple-element.12), channel_id=1, source_target_pairs={{0,1},{1,0},{2,3},{3,2},{4,5},{5,4},{6,7},{7,6},{8,9},{9,8},{10,11... | collective-permute-start | bytes 1572872 | tf_op jit(solution)/shard_map/window_gather/ppermute | solution.py:62
  137.0 9.5 %all-to-all-start.5 = ((f32[8,2,16,256]{3,2,1,0:T(8,128)}), f32[8,2,16,256]{3,2,1,0:T(8,128)S(1)}, u32[]{:S(2)}, u32[]{:S(2)}) async-start(f32[8,2,16,256]{3,2,1,0:T(8,128)} %broadcast_in_dim.20), calls=%async_computation.5 | async-start | bytes 524288 | tf_op jit(solution)/shard_map/weight_sum/all_to_all | solution.py:68
  146.5 17.4 %all-to-all-start.1 = ((bf16[8,256,256]{2,1,0:T(8,128)(2,1)}), bf16[8,256,256]{2,1,0:T(8,128)(2,1)S(1)}, u32[]{:S(2)}, u32[]{:S(2)}) async-start(bf16[8,256,256]{2,1,0:T(8,128)(2,1)} %bitcast.14), calls=%async_computation.1 | async-start | bytes 2097152 | tf_op jit(solution)/shard_map/source_sum/all_to_all | solution.py:168
